TPU v7x, 256 devices: a whole 4x4x8 slice. The times are simulated.
256 devices in a mesh: dp: 32 (over z_lo, x, core), rows: 8 (over z_hi, y).
Axes of the slice: x: 4, y: 4, z: 8 (z_hi: 2, z_lo: 4; z = z_hi * 4 + z_lo), core: 2. Of those that a mesh axis runs over, the one named last changes fastest.
Arguments:
- features: bfloat16 [64, 48, 64, 1024], P('dp', 'rows'), may hold values from -8 to 8
- first_atrous_weight: bfloat16 [3, 3, 1024, 256], P(None, None, 'dp'), may hold values from -0.0625 to 0.0625
- second_atrous_weight: bfloat16 [3, 3, 1024, 256], P(None, None, 'dp'), may hold values from -0.0625 to 0.0625
- third_atrous_weight: bfloat16 [3, 3, 1024, 256], P(None, None, 'dp'), may hold values from -0.0625 to 0.0625
- pointwise_weight: bfloat16 [1024, 256], replicated, may hold values from -0.1875 to 0.1875
- pooling_weight: bfloat16 [1024, 256], replicated, may hold values from -0.1875 to 0.1875
- projection_weight: bfloat16 [1280, 256], replicated, may hold values from -0.15625 to 0.15625
- branch_norm_gain: float32 [4, 256], replicated, may hold values from 0.25 to 1.75
- branch_norm_shift: float32 [4, 256], replicated, may hold values from -3 to 3
- projection_norm_gain: float32 [256], replicated, may hold values from 0.25 to 1.75
- projection_norm_shift: float32 [256], replicated, may hold values from -3 to 3
- ghost_group_index: int32 [64], replicated, may hold values from 0 to 15, as said below
Outputs:
- decoder_in: bfloat16 [64, 48, 64, 256], P(None, 'rows', 'dp')
Inputs may be any that keep to these rules, and one draw needn't show every extreme that they name: `ghost_group_index`: each of the 16 group ids names exactly 4 images.
All inputs are finite; a program needn't handle non-finite values.
Results may differ from a plain program's by a relative error of at most 0.0014.
The roundings to bfloat16 on the way count: a program that leaves them out, or rounds other values in their place, can miss the bound.
Values may be sent and summed in bfloat16 or wider, within the bound.
A program may use at most 128 MiB of HBM per device.

v0:
```python
import jax
import jax.numpy as jnp
from jax import lax
from jax.sharding import PartitionSpec as P

DILATION_FIRST = 12
DILATION_SECOND = 24
DILATION_THIRD = 36


def from_behind(array, axis, by):
    count = lax.axis_size(axis)
    pairs = [(i, i + by) for i in range(count) if 0 <= i + by < count]
    return lax.ppermute(array, axis, pairs)


def row_tap_list(block_tensor, kernel_row_slice, dilation_rate):
    partial_terms = jnp.einsum(
        "irwc,kco->irwko", block_tensor, kernel_row_slice, preferred_element_type=jnp.float32
    )
    map_width = block_tensor.shape[2]
    left_padding = jnp.pad(partial_terms[:, :, :, 0], ((0, 0), (0, 0), (dilation_rate, 0), (0, 0)))[
        :, :, :map_width
    ]
    right_padding = jnp.pad(
        partial_terms[:, :, :, 2], ((0, 0), (0, 0), (0, dilation_rate), (0, 0))
    )[:, :, dilation_rate:]
    return partial_terms[:, :, :, 1] + left_padding + right_padding


def dilated_result(features, kernel_weight, dilation_rate):
    step_offsets = dilation_rate // features.shape[1]
    running_sum = row_tap_list(features, kernel_weight[1], dilation_rate)
    for by_dev, tap_offset in ((step_offsets, 0), (-step_offsets, 2)):
        shifted_rows = from_behind(features, "rows", by_dev)
        running_sum = running_sum + row_tap_list(
            shifted_rows, kernel_weight[tap_offset], dilation_rate
        )
    return running_sum


def stats_terms(pre, onehot):
    first = jnp.sum(pre, axis=(1, 2))
    second = jnp.sum(pre * pre, axis=(1, 2))
    group_first = jnp.dot(onehot.T, first, precision=lax.Precision.HIGHEST)
    group_second = jnp.dot(onehot.T, second, precision=lax.Precision.HIGHEST)
    return (group_first, group_second)


def apply_norm(pre, onehot, total_first, total_second, count, gain, shift):
    mean = total_first / count
    var = total_second / count - mean * mean
    inv = lax.rsqrt(var + 1e-05)
    img_mean = jnp.dot(onehot, mean, precision=lax.Precision.HIGHEST)
    img_inv = jnp.dot(onehot, inv, precision=lax.Precision.HIGHEST)
    scaled = (pre - img_mean[:, None, None, :]) * img_inv[:, None, None, :] * gain + shift
    return jax.nn.relu(scaled).astype(jnp.bfloat16)


def project(joined, onehot, projection_weight, count, projection_norm_gain, projection_norm_shift):
    proj = jnp.einsum(
        "irwc,co->irwo", joined, projection_weight, preferred_element_type=jnp.float32
    )
    group_first, group_second = stats_terms(proj, onehot)
    total_first, total_second = lax.psum((group_first, group_second), ("dp", "rows"))
    return apply_norm(
        proj, onehot, total_first, total_second, count, projection_norm_gain, projection_norm_shift
    )


def shards(
    features,
    first_atrous_weight,
    second_atrous_weight,
    third_atrous_weight,
    pointwise_weight,
    pooling_weight,
    projection_weight,
    branch_norm_gain,
    branch_norm_shift,
    projection_norm_gain,
    projection_norm_shift,
    ghost_group_index,
):
    img_dev, rows_dev, cols, chans = features.shape
    dp_size = lax.axis_size("dp")
    rows_size = lax.axis_size("rows")
    images = img_dev * dp_size
    groups = images // 4
    pixels = rows_dev * rows_size * cols
    count = 4.0 * pixels
    start = lax.axis_index("dp") * img_dev
    labels = jnp.arange(groups, dtype=jnp.int32)
    all_hot = (ghost_group_index[:, None] == labels[None, :]).astype(jnp.float32)
    own_hot = lax.dynamic_slice_in_dim(all_hot, start, img_dev, 0)
    first_kernel, second_kernel, third_kernel = (
        lax.all_gather(first_atrous_weight, "dp", axis=2, tiled=True),
        lax.all_gather(second_atrous_weight, "dp", axis=2, tiled=True),
        lax.all_gather(third_atrous_weight, "dp", axis=2, tiled=True),
    )
    pointwise_output = jnp.einsum(
        "irwc,co->irwo", features, pointwise_weight, preferred_element_type=jnp.float32
    )
    pre = jnp.concatenate(
        [
            pointwise_output,
            dilated_result(features, first_kernel, DILATION_FIRST),
            dilated_result(features, second_kernel, DILATION_SECOND),
            dilated_result(features, third_kernel, DILATION_THIRD),
        ],
        -1,
    )
    group_first, group_second = stats_terms(pre, own_hot)
    pool_part = jnp.sum(features, axis=(1, 2), dtype=jnp.float32)
    pool_total = lax.psum(pool_part, "rows")
    total_first, total_second = lax.psum((group_first, group_second), ("dp", "rows"))
    branches = apply_norm(
        pre,
        own_hot,
        total_first,
        total_second,
        count,
        branch_norm_gain.reshape(-1),
        branch_norm_shift.reshape(-1),
    )
    pooled = (pool_total / pixels).astype(jnp.bfloat16)
    pool_act = jax.nn.relu(
        jnp.dot(pooled, pooling_weight, preferred_element_type=jnp.float32)
    ).astype(jnp.bfloat16)
    pool_map = jnp.broadcast_to(
        pool_act[:, None, None, :], (img_dev, rows_dev, cols, pool_act.shape[1])
    )
    joined = jnp.concatenate([branches, pool_map], -1)
    local_out = project(
        joined, own_hot, projection_weight, count, projection_norm_gain, projection_norm_shift
    )
    return lax.all_to_all(local_out, "dp", split_axis=2, concat_axis=0, tiled=True)


def solution(mesh):
    in_specs = (
        P("dp", "rows", None, None),
        P(None, None, "dp", None),
        P(None, None, "dp", None),
        P(None, None, "dp", None),
        P(),
        P(),
        P(),
        P(),
        P(),
        P(),
        P(),
        P(),
    )
    out_specs = P(None, "rows", "dp", None)
    return jax.shard_map(shards, mesh=mesh, in_specs=in_specs, out_specs=out_specs, check_vma=False)
```

profile of v0, /device:TPU:1, one launch (start us, length us, event | category | flops | bytes accessed | tf_op | source)
XLA Modules:
  0.0 726.8 jit_solution(7017526560821502395)
XLA Ops:
  6.5 0.7 all-gather.4.cloned.1.call-update
  7.3 0.7 all-gather.6.cloned.1.call-update
  8.1 0.7 all-gather.8.cloned.1.call-update
  8.8 1.3 collective-permute-start.1
  10.1 7.5 %collective-permute-start = (bf16[2,6,64,1024]{3,2,1,0:T(8,128)(2,1)}, bf16[2,6,64,1024]{3,2,1,0:T(8,128)(2,1)}, u32[]{:S(2)}, u32[]{:S(2)}) collective-permute-start(bf16[2,6,64,1024]{3,2,1,0:T(8,128)(2,1)} %param.12), channel_id=1, source_target_pairs={{0,2},{1,3},{2,4},{3,5},{4,6},{5,7},{8,10},{9,11},{10,12},{11,13},... | collective-permute-start | bytes 4718600 | tf_op jit(solution)/shard_map/ppermute | solution.py:14
  17.6 1.3 collective-permute-start.3
  18.9 11.2 %collective-permute-start.2 = (bf16[2,6,64,1024]{3,2,1,0:T(8,128)(2,1)}, bf16[2,6,64,1024]{3,2,1,0:T(8,128)(2,1)}, u32[]{:S(2)}, u32[]{:S(2)}) collective-permute-start(bf16[2,6,64,1024]{3,2,1,0:T(8,128)(2,1)} %param.12), channel_id=1, source_target_pairs={{0,4},{1,5},{2,6},{3,7},{8,12},{9,13},{10,14},{11,15},{16,20},{17,... | collective-permute-start | bytes 4718600 | tf_op jit(solution)/shard_map/ppermute | solution.py:14
  30.1 1.3 collective-permute-start.5
  31.4 0.7 dynamic-slice
  32.1 1.7 convert_reduce_fusion
  33.9 146.7 %psum.37 = f32[2,1024]{1,0:T(2,128)S(1)} all-reduce(f32[2,1024]{1,0:T(2,128)S(1)} %convert_reduce_fusion), channel_id=1, replica_groups=mesh['dp'=32,'rows'=8] {'rows'}, use_global_device_ids=true, to_apply=%region_5.6 | all-reduce | flops 2048 | bytes 16384 | tf_op jit(solution)/shard_map/psum | solution.py:115
  180.5 2.1 fusion.49
  182.7 2.4 collective-permute-start.4
  185.1 3.4 fusion.10
  188.5 1.4 slice_bitcast_fusion.36
  189.9 2.8 fusion.11
  192.7 1.4 slice_bitcast_fusion.39
  194.1 1.4 fusion.12
  195.5 1.3 slice_bitcast_fusion.42
  196.8 0.6 copy-done.17
  197.4 90.0 %all-gather.6.cloned.1.call-done = bf16[3,3,1024,256]{3,2,1,0:T(8,128)(2,1)} async-done(((bf16[3,3,32,256]{3,2,1,0:T(8,128)(2,1)}), bf16[3,3,1024,256]{3,2,1,0:T(8,128)(2,1)}) %all-gather.6.cloned.1.call-update) | async-done | bytes 4718608 | tf_op jit(solution)/shard_map/all_gather | solution.py:98
  287.4 3.4 fusion.7
  290.8 1.4 slice_bitcast_fusion.27
  292.3 2.8 fusion.8
  295.1 1.4 slice_bitcast_fusion.30
  296.5 1.4 fusion.9
  297.9 1.5 slice_bitcast_fusion.33
  299.8 61.1 %all-gather.8.cloned.1.call-done = bf16[3,3,1024,256]{3,2,1,0:T(8,128)(2,1)} async-done(((bf16[3,3,32,256]{3,2,1,0:T(8,128)(2,1)}), bf16[3,3,1024,256]{3,2,1,0:T(8,128)(2,1)}) %all-gather.8.cloned.1.call-update) | async-done | bytes 4718608 | tf_op jit(solution)/shard_map/all_gather | solution.py:99
  361.0 3.4 fusion.4
  364.5 2.8 fusion.5
  367.5 1.4 fusion.6
  369.1 0.9 copy-done.3
  370.8 2.3 fusion.26
  373.8 1.9 fusion.34
  375.7 0.6 fusion.42
  376.3 0.9 copy-done.1
  377.6 0.9 fusion.79
  378.5 0.9 fusion.78
  379.6 0.7 copy.119
  380.3 0.7 copy.120
  381.0 237.9 %all-reduce.22.cloned.1.call-done = (f32[16,1024]{1,0:T(8,128)}, f32[16,1024]{1,0:T(8,128)}) async-done(((f32[16,1024]{1,0:T(8,128)}, f32[16,1024]{1,0:T(8,128)}), (f32[16,1024]{1,0:T(8,128)}, f32[16,1024]{1,0:T(8,128)})) %all-reduce.22.cloned.1.call-update) | async-done | bytes 131088 | tf_op jit(solution)/shard_map/psum | solution.py:116
  618.9 1.0 fusion.58
  620.0 1.1 fusion.51
  621.0 1.7 maximum_convert_fusion
  622.8 0.7 fusion.96
  624.1 76.6 %all-reduce.18 = (f32[16,256]{1,0:T(8,128)S(1)}, f32[16,256]{1,0:T(8,128)S(1)}) all-reduce(f32[16,256]{1,0:T(8,128)S(1)} %fusion.76, f32[16,256]{1,0:T(8,128)S(1)} %fusion.77), channel_id=1, replica_groups=mesh['dp'=32,'rows'=8] {'dp','rows'}, use_global_device_ids=true, to_apply=%region_9.10 | all-reduce | flops 8192 | bytes 65536 | tf_op jit(solution)/shard_map/psum | solution.py:65
  701.6 17.6 %all_to_all.18 = bf16[2,6,64,256]{3,0,1,2:T(2,128)(2,1)S(1)} all-to-all(bf16[2,6,64,256]{3,0,1,2:T(2,128)(2,1)S(1)} %copy.97), channel_id=1, replica_groups=mesh['dp'=32,'rows'=8] {'dp'}, dimensions={2} | all-to-all | bytes 786432 | tf_op jit(solution)/shard_map/all_to_all | solution.py:137
  719.3 1.0 copy.98
  (75 shorter events, 4.6 us)
Async XLA Ops:
  6.5 616.3 %copy-start = (bf16[1280,256]{1,0:T(8,128)(2,1)S(1)}, bf16[1280,256]{1,0:T(8,128)(2,1)}, u32[]{:S(2)}) copy-start(bf16[1280,256]{1,0:T(8,128)(2,1)} %param.18) | copy-start | bytes 1966084
  6.5 178.6 %all-gather.4.cloned.1.call-start = ((), (), s32[]{:S(2)}) async-start(), calls=%async_computation.1 | async-start | bytes 4866048 | tf_op jit(solution)/shard_map/all_gather | solution.py:97
  7.3 280.2 %all-gather.6.cloned.1.call-start = ((), (), s32[]{:S(2)}) async-start(), calls=%async_computation.2 | async-start | bytes 4866048 | tf_op jit(solution)/shard_map/all_gather | solution.py:98
  8.0 174.6 %copy-start.2 = (bf16[2,6,64,1024]{3,2,1,0:T(8,128)(2,1)S(1)}, bf16[2,6,64,1024]{3,2,1,0:T(8,128)(2,1)}, u32[]{:S(2)}) copy-start(bf16[2,6,64,1024]{3,2,1,0:T(8,128)(2,1)} %param.12) | copy-start | bytes 4718596
  8.0 352.9 %all-gather.8.cloned.1.call-start = ((), (), s32[]{:S(2)}) async-start(), calls=%async_computation.3 | async-start | bytes 4866048 | tf_op jit(solution)/shard_map/all_gather | solution.py:99
  8.8 610.2 %all-reduce.22.cloned.1.call-start = ((), (), s32[]{:S(2)}) async-start(), calls=%async_computation.4 | async-start | bytes 262144 | tf_op jit(solution)/shard_map/psum | solution.py:116
  8.8 173.8 %collective-permute-start.1 = (bf16[2,6,64,1024]{3,2,1,0:T(8,128)(2,1)}, bf16[2,6,64,1024]{3,2,1,0:T(8,128)(2,1)}, u32[]{:S(2)}, u32[]{:S(2)}) collective-permute-start(bf16[2,6,64,1024]{3,2,1,0:T(8,128)(2,1)} %param.12), channel_id=1, source_target_pairs={{2,0},{3,1},{4,2},{5,3},{6,4},{7,5},{10,8},{11,9},{12,10},{13,11},... | collective-permute-start | bytes 4718600 | tf_op jit(solution)/shard_map/ppermute | solution.py:14
  10.1 179.8 %collective-permute-start = (bf16[2,6,64,1024]{3,2,1,0:T(8,128)(2,1)}, bf16[2,6,64,1024]{3,2,1,0:T(8,128)(2,1)}, u32[]{:S(2)}, u32[]{:S(2)}) collective-permute-start(bf16[2,6,64,1024]{3,2,1,0:T(8,128)(2,1)} %param.12), channel_id=1, source_target_pairs={{0,2},{1,3},{2,4},{3,5},{4,6},{5,7},{8,10},{9,11},{10,12},{11,13},... | collective-permute-start | bytes 4718600 | tf_op jit(solution)/shard_map/ppermute | solution.py:14
  17.6 179.9 %collective-permute-start.3 = (bf16[2,6,64,1024]{3,2,1,0:T(8,128)(2,1)}, bf16[2,6,64,1024]{3,2,1,0:T(8,128)(2,1)}, u32[]{:S(2)}, u32[]{:S(2)}) collective-permute-start(bf16[2,6,64,1024]{3,2,1,0:T(8,128)(2,1)} %param.12), channel_id=1, source_target_pairs={{4,0},{5,1},{6,2},{7,3},{12,8},{13,9},{14,10},{15,11},{20,16},{21,... | collective-permute-start | bytes 4718600 | tf_op jit(solution)/shard_map/ppermute | solution.py:14
  18.9 273.4 %collective-permute-start.2 = (bf16[2,6,64,1024]{3,2,1,0:T(8,128)(2,1)}, bf16[2,6,64,1024]{3,2,1,0:T(8,128)(2,1)}, u32[]{:S(2)}, u32[]{:S(2)}) collective-permute-start(bf16[2,6,64,1024]{3,2,1,0:T(8,128)(2,1)} %param.12), channel_id=1, source_target_pairs={{0,4},{1,5},{2,6},{3,7},{8,12},{9,13},{10,14},{11,15},{16,20},{17,... | collective-permute-start | bytes 4718600 | tf_op jit(solution)/shard_map/ppermute | solution.py:14
  30.1 269.7 %collective-permute-start.5 = (bf16[2,6,64,1024]{3,2,1,0:T(8,128)(2,1)}, bf16[2,6,64,1024]{3,2,1,0:T(8,128)(2,1)}, u32[]{:S(2)}, u32[]{:S(2)}) collective-permute-start(bf16[2,6,64,1024]{3,2,1,0:T(8,128)(2,1)} %param.12), channel_id=1, source_target_pairs={{6,0},{7,1},{14,8},{15,9},{22,16},{23,17},{30,24},{31,25},{38,32},... | collective-permute-start | bytes 4718600 | tf_op jit(solution)/shard_map/ppermute | solution.py:14
  182.7 181.9 %collective-permute-start.4 = (bf16[2,6,64,1024]{3,2,1,0:T(8,128)(2,1)S(1)}, bf16[2,6,64,1024]{3,2,1,0:T(8,128)(2,1)}, u32[]{:S(2)}, u32[]{:S(2)}) collective-permute-start(bf16[2,6,64,1024]{3,2,1,0:T(8,128)(2,1)S(1)} %copy-done.2), channel_id=1, source_target_pairs={{0,6},{1,7},{8,14},{9,15},{16,22},{17,23},{24,30},{25,31},{32,38},... | collective-permute-start | bytes 4718600 | tf_op jit(solution)/shard_map/ppermute | solution.py:14
  185.1 4.8 copy-start.26
  188.5 4.2 copy-start.15
  192.7 2.8 copy-start.16
  195.5 2.0 copy-start.17
  287.4 4.8 copy-start.25
  290.8 4.2 copy-start.18
  295.1 2.8 copy-start.19
  297.9 2.0 copy-start.20
  361.0 3.6 copy-start.24
  367.5 1.6 copy-start.7
  367.5 1.6 copy-start.8
  368.9 1.1 copy-start.3
  368.9 1.4 copy-start.4
  368.9 1.6 copy-start.5
  368.9 1.8 copy-start.6
  370.8 2.3 copy-start.9
  370.8 2.3 copy-start.10
  370.8 2.3 copy-start.11
  370.8 2.5 copy-start.12
  370.8 2.8 copy-start.13
  370.8 3.0 copy-start.14
  376.3 0.9 copy-start.1
  377.2 2.2 copy-start.21
  622.8 78.2 %copy-start.22 = (f32[256]{0:T(256)S(1)}, f32[256]{0:T(256)}, u32[]{:S(2)}) copy-start(f32[256]{0:T(256)} %param.22) | copy-start | bytes 3076
  622.8 78.2 %copy-start.23 = (f32[256]{0:T(256)S(1)}, f32[256]{0:T(256)}, u32[]{:S(2)}) copy-start(f32[256]{0:T(256)} %param.21) | copy-start | bytes 3076
Sparse Core Ops, SparseCore 0:
  9.2 144.8 all-gather.3
  156.0 131.4 all-gather.5
  289.3 71.6 all-gather.7
  379.6 239.3 all-reduce.21
where the time goes:
time: 728 us; the launch traced here: 727 us
  waiting for transfers between devices  391 us (54%)
  blocking collectives  241 us (33%)
  matrix products  30.6 us (4%)
  starting transfers between devices  25.1 us (3%)
  local copies, waits for them, and re-layouts  16.8 us (2%)
  between operations  13.6 us (2%)
  other arithmetic  8.76 us (1%)
    psum x1, waiting for transfers between devices, shards(): lax.psum((group_first, group_second), ('dp', 'rows'))  238 us
    psum x1, blocking collectives, shards(): pool_total = lax.psum(pool_part, 'rows')  147 us
    all_gather x1, waiting for transfers between devices, shards(): lax.all_gather(second_atrous_weight, 'dp', axis=2, tiled=True)  90 us
    psum x1, blocking collectives, project(): lax.psum((group_first, group_second), ('dp', 'rows'))  76.6 us
    all_gather x1, waiting for transfers between devices, shards(): lax.all_gather(third_atrous_weight, 'dp', axis=2, tiled=True)  61.1 us
    ppermute x6, starting transfers between devices, from_behind(): return lax.ppermute(array, axis, pairs)  25 us
    dot_general x9, matrix products, row_tap_list(): jnp.einsum('irwc,kco->irwko', block_tensor, kernel_row_slice, preferred_e...  22.8 us
    all_to_all x1, blocking collectives, shards(): lax.all_to_all(local_out, 'dp', split_axis=2, concat_axis=0, tiled=True)  17.6 us
  transfers between devices with their start and end apart: 10, of which 3 were waited for; matrix products, arithmetic and copies ran while one was open for 5% of the time, Pallas kernels for 0%

commit v1 on v0

v1 whole, which is shorter than its diff:
```python
import functools

import jax
import jax.numpy as jnp
from jax import lax
from jax.experimental import pallas as pl
from jax.experimental.pallas import tpu as pltpu
from jax.sharding import PartitionSpec as P

MESH = pl.DeviceIdType.MESH
F32 = jnp.float32
BF16 = jnp.bfloat16
ORDER = ((0, 1), (1, 1), (2, 1), (0, 0), (0, 2), (1, 0), (1, 2), (2, 0), (2, 2))
CHUNKS = len(ORDER)
COUNT = 4.0 * 48 * 64
PIXELS = 48.0 * 64


def device(x, y, z, c):
    x, y, z, c = lax.rem(x + 4, 4), lax.rem(y + 4, 4), lax.rem(z + 8, 8), lax.rem(c, 2)
    return (lax.rem(z, 4) * 8 + x * 2 + c, (z // 4) * 4 + y)


def remote(src, dst, send, recv, to):
    return pltpu.make_async_remote_copy(
        src_ref=src, dst_ref=dst, send_sem=send, recv_sem=recv, device_id=to, device_id_type=MESH
    )


def kernel(
    feat, wa, wb, wc, point_w, pool_w, proj_w, gain, shift, pgain, pshift, group,
    out,
    wbuf, xbuf, xright, xleft, acc, proj, rows, tiles, sendbuf, pool_buf,
    msg_a, got_a, red_a, sum_y_a, sum_z_a, all_a,
    msg_b, got_b, red_b, sum_y_b, sum_z_b, all_b,
    local_sem, ws, wr, fs, fr, ps, pr, as_a, ar_a, as_b, ar_b, end_send, end_recv,
):
    d, r = lax.axis_index("dp"), lax.axis_index("rows")
    z_lo, x, c = d // 8, lax.rem(d // 2, 4), lax.rem(d, 2)
    z_hi, y = r // 4, lax.rem(r, 4)
    z = z_hi * 4 + z_lo
    parity, half = lax.rem(y, 2), y // 2
    own = z_hi * 2 + half
    image = (d // 2) * 4 + own
    other = 1 - c
    y_pair = y + 1 - 2 * parity
    up, down = device(x, y, z + 1, c), device(x, y, z - 1, c)
    right, left = device(x + 1, y, z, c), device(x - 1, y, z, c)
    sibling = device(x, y, z, other)
    pool_peers = (sibling, device(x, y_pair, z, c), device(x, y_pair, z, other))

    locals_ = [
        pltpu.make_async_copy(w, wbuf.at[pl.ds(9 * i, 9), z_lo, x, c], local_sem.at[i])
        for i, w in enumerate((wa, wb, wc))
    ]
    for cp in locals_:
        cp.start()

    barrier = pltpu.get_barrier_semaphore()
    for peer in (up, down, right, left) + pool_peers:
        pl.semaphore_signal(barrier, inc=1, device_id=peer, device_id_type=MESH)
    for b in range(4):
        src = device(x, 2 * (b % 2) + parity, (b // 2) * 4 + z_lo, z_hi)

        @pl.when(jnp.logical_not(jnp.logical_and(own == b, c == z_hi)))
        def _():
            pl.semaphore_signal(barrier, inc=1, device_id=src, device_id_type=MESH)

    @pl.when(c == z_hi)
    def _():
        pl.semaphore_wait(barrier, 10)

    @pl.when(c != z_hi)
    def _():
        pl.semaphore_wait(barrier, 11)

    for cp in locals_:
        cp.wait()

    def taps(k):
        b, kh = ORDER[k]
        return pl.ds(9 * b + 3 * kh, 3)

    def shard(k, zz, rows=None):
        ref = wbuf.at[taps(k), zz, x, c]
        return ref if rows is None else wbuf.at[taps(k), zz, x, c, pl.ds(rows, 16)]

    def column(k, xx, cc, zs=None):
        return wbuf.at[taps(k), slice(None) if zs is None else pl.ds(zs, 2), xx, cc]

    z_next, z_prev = lax.rem(z_lo + 1, 4), lax.rem(z_lo + 3, 4)
    z_far = lax.rem(z_lo + 2, 4)
    x_next, x_prev, x_far = lax.rem(x + 1, 4), lax.rem(x + 3, 4), lax.rem(x + 2, 4)

    def to(ref, k, i, peer):
        return remote(ref, ref, ws.at[k, i], wr.at[k, i], peer)

    sent = []

    def send(ref, k, i, peer):
        cp = to(ref, k, i, peer)
        cp.start()
        sent.append(cp)

    def arrived(ref, k, i):
        to(ref, k, i, sibling).wait_recv()

    for k in range(2):
        send(shard(k, z_lo), k, 0, up)
        send(shard(k, z_lo), k, 1, down)

    for i in range(2):
        for h in range(2):
            src = feat.at[i, pl.ds(3 * h, 3)]
            is_self = jnp.logical_and(jnp.logical_and(c == z_hi, c == h), half == i)

            @pl.when(is_self)
            def _():
                pltpu.make_async_copy(src, xbuf.at[own], fr.at[own]).start()

            @pl.when(jnp.logical_not(is_self))
            def _():
                remote(
                    src, xbuf.at[own], fs.at[2 * i + h], fr.at[own],
                    device(x, 2 * i + parity, c * 4 + z_lo, jnp.int32(h)),
                ).start()

    for k in range(2, CHUNKS):
        send(shard(k, z_lo), k, 0, up)
        send(shard(k, z_lo), k, 1, down)

    def features_arrive():
        for b in range(4):
            pltpu.make_async_copy(xbuf.at[b], xbuf.at[b], fr.at[b]).wait()
        part = jnp.zeros((8, 1024), F32)
        col = lax.broadcasted_iota(jnp.int32, (64, 1024), 0)

        def body(t, part):
            v = xbuf[t // 3, lax.rem(t, 3)].astype(F32)
            xright[t // 3, lax.rem(t, 3)] = jnp.where(col >= 4, pltpu.roll(v, 4, 0), 0.0).astype(BF16)
            xleft[t // 3, lax.rem(t, 3)] = jnp.where(col < 60, pltpu.roll(v, 60, 0), 0.0).astype(BF16)
            return part + v.reshape(8, 8, 1024).sum(axis=0)

        pool_buf[0] = lax.fori_loop(0, 12, body, part)
        for i, peer in enumerate(pool_peers):
            remote(pool_buf.at[0], pool_buf.at[i + 1], ps.at[i], pr.at[i], peer).start()

        def point(b, _):
            acc[b, :, :, 0:256] = jnp.dot(
                xbuf[b].reshape(192, 1024), point_w[...], preferred_element_type=F32
            ).reshape(3, 64, 256)
            return 0

        lax.fori_loop(0, 4, point, 0)

    def compute(k):
        branch, kh = ORDER[k]
        step = branch + 1
        x0 = (0, 0, step)[kh]
        o0 = (step, 0, 0)[kh]
        blocks = 4 if kh == 1 else 4 - step
        lanes = slice(256 * (branch + 1), 256 * (branch + 2))

        def body(t, _):
            b, o = x0 + t, o0 + t

            def times(lhs, kw):
                n = lhs.shape[1]
                w = wbuf[9 * branch + 3 * kh + kw].reshape(1024, 256)
                return jnp.dot(
                    lhs.reshape(3 * n, 1024), w, preferred_element_type=F32
                ).reshape(3, n, 256)

            mid = times(xbuf[b], 1)
            if kh == 1:
                acc[o, :, :, lanes] = mid
            else:
                acc[o, :, :, lanes] += mid
            if branch == 0:
                acc[o, :, 8:64, lanes] += times(xright[b], 0)[:, 0:56]
                acc[o, :, 0:56, lanes] += times(xleft[b], 2)[:, 8:64]
            elif branch == 1:
                acc[o, :, 24:64, lanes] += times(xbuf[b, :, 0:48], 0)[:, 0:40]
                acc[o, :, 0:40, lanes] += times(xbuf[b, :, 16:64], 2)[:, 8:48]
            else:
                acc[o, :, 32:64, lanes] += times(xright[b, :, 0:32], 0)
                acc[o, :, 0:32, lanes] += times(xleft[b, :, 32:64], 2)
            return 0

        lax.fori_loop(0, blocks, body, 0)

    for t in range(CHUNKS + 4):
        k = t
        if 0 <= k < CHUNKS:
            arrived(shard(k, z_prev), k, 0)
            send(shard(k, z_prev, 16), k, 2, up)
            arrived(shard(k, z_next), k, 1)
            send(shard(k, z_next, 0), k, 3, down)
        k = t - 1
        if 0 <= k < CHUNKS:
            arrived(shard(k, z_far, 16), k, 2)
            arrived(shard(k, z_far, 0), k, 3)
            send(column(k, x, c), k, 4, right)
            send(column(k, x, c), k, 5, left)
            send(column(k, x, c), k, 8, sibling)
        k = t - 2
        if 0 <= k < CHUNKS:
            arrived(column(k, x_prev, c), k, 4)
            send(column(k, x_prev, c, 2), k, 6, right)
            arrived(column(k, x_next, c), k, 5)
            send(column(k, x_next, c, 0), k, 7, left)
            send(column(k, x_prev, c), k, 9, sibling)
            send(column(k, x_next, c), k, 10, sibling)
        k = t - 3
        if 0 <= k < CHUNKS:
            arrived(column(k, x_far, c, 2), k, 6)
            arrived(column(k, x_far, c, 0), k, 7)
            send(column(k, x_far, c), k, 11, sibling)
        if t == 7:
            features_arrive()
        for k in (2 * (t - 8), 2 * (t - 8) + 1):
            if 0 <= k < CHUNKS:
                arrived(column(k, x, other), k, 8)
                arrived(column(k, x_prev, other), k, 9)
                arrived(column(k, x_next, other), k, 10)
                arrived(column(k, x_far, other), k, 11)
                compute(k)

    for cp in sent:
        cp.wait_send()

    mine = group[image]
    spot = x * 2 + c

    def all_reduce(msg, got, red, sum_y, sum_z, full, s_sem, r_sem):
        def peer(o):
            s = lax.rem(spot + o, 8)
            return s, device(s // 2, y, z, lax.rem(s, 2))

        copies = []

        def go(src, dst, i, to_):
            cp = remote(src, dst, s_sem.at[i], r_sem.at[i], to_)
            cp.start()
            copies.append(cp)

        for o in range(1, 8):
            s, to_ = peer(o)
            go(msg.at[s], got.at[o - 1], o - 1, to_)
        total = msg[spot]
        for o in range(1, 8):
            copies[o - 1].wait_recv()
            total = total + got[o - 1]
        red[0] = total
        for o in range(1, 4):
            go(red.at[0], sum_y.at[o - 1], 6 + o, device(x, y + o, z, c))
        for o in range(1, 4):
            copies[6 + o].wait_recv()
            total = total + sum_y[o - 1]
        red[1] = total
        for o in range(1, 8):
            go(red.at[1], sum_z.at[o - 1], 9 + o, device(x, y, z + o, c))
        for o in range(1, 8):
            copies[9 + o].wait_recv()
            total = total + sum_z[o - 1]
        full[spot] = total
        for o in range(1, 8):
            s, to_ = peer(o)
            go(full.at[spot], full.at[spot], 16 + o, to_)
        for o in range(1, 8):
            s = lax.rem(spot - o + 8, 8)
            remote(full.at[s], full.at[s], s_sem.at[16 + o], r_sem.at[16 + o], sibling).wait_recv()
        return copies

    def add_up(t, carry):
        first, second = carry
        v = acc[t // 3, lax.rem(t, 3)].reshape(8, 8, 1024)
        return first + v.sum(axis=0), second + (v * v).sum(axis=0)

    zero = jnp.zeros((8, 1024), F32)
    first, second = lax.fori_loop(0, 12, add_up, (zero, zero))
    first = jnp.sum(first, axis=0, keepdims=True)
    second = jnp.sum(second, axis=0, keepdims=True)
    labels = lax.broadcasted_iota(jnp.int32, (16, 128), 0)
    for s in range(8):
        lanes = slice(128 * s, 128 * (s + 1))
        msg_a[s, 0:16] = jnp.where(labels == mine, first[:, lanes], 0.0)
        msg_a[s, 16:32] = jnp.where(labels == mine, second[:, lanes], 0.0)
    waits = all_reduce(msg_a, got_a, red_a, sum_y_a, sum_z_a, all_a, as_a, ar_a)

    means, invs = [], []
    for s in range(8):
        g1 = jnp.sum(jnp.where(labels == mine, all_a[s, 0:16], 0.0), axis=0, keepdims=True)
        g2 = jnp.sum(jnp.where(labels == mine, all_a[s, 16:32], 0.0), axis=0, keepdims=True)
        mean = g1 / COUNT
        means.append(mean)
        invs.append(lax.rsqrt(g2 / COUNT - mean * mean + 1e-05))
    mean = jnp.concatenate(means, axis=1)
    inv = jnp.concatenate(invs, axis=1)

    for i in range(3):
        remote(pool_buf.at[i + 1], pool_buf.at[i + 1], ps.at[i], pr.at[i], sibling).wait()
    pool = pool_buf[0] + pool_buf[1] + pool_buf[2] + pool_buf[3]
    pooled = (jnp.sum(pool, axis=0, keepdims=True) / PIXELS).astype(BF16)
    pooled = jnp.broadcast_to(pooled, (16, 1024))
    act = jnp.maximum(jnp.dot(pooled, pool_w[...], preferred_element_type=F32), 0.0).astype(BF16)
    pool_row = jnp.dot(act, proj_w[1024:1280], preferred_element_type=F32)[0:1]

    def project(b, carry):
        first, second = carry
        v = acc[b].reshape(192, 1024)
        v = (v - mean) * inv * gain[...] + shift[...]
        v = jnp.maximum(v, 0.0).astype(BF16)
        p = jnp.dot(v, proj_w[0:1024], preferred_element_type=F32) + pool_row
        proj[b] = p
        p = p.reshape(24, 8, 256)
        return first + p.sum(axis=0), second + (p * p).sum(axis=0)

    zero = jnp.zeros((8, 256), F32)
    first, second = lax.fori_loop(0, 4, project, (zero, zero))
    first = jnp.sum(first, axis=0, keepdims=True)
    second = jnp.sum(second, axis=0, keepdims=True)
    row = lax.broadcasted_iota(jnp.int32, (8, 128), 0)
    kind = lax.rem(row, 4)
    base = jnp.where(
        kind == 0, first[:, 0:128],
        jnp.where(kind == 1, first[:, 128:256], jnp.where(kind == 2, second[:, 0:128], second[:, 128:256])),
    )
    for s in range(8):
        msg_b[s] = jnp.where(2 * s + row // 4 == mine, base, 0.0)
    waits += all_reduce(msg_b, got_b, red_b, sum_y_b, sum_z_b, all_b, as_b, ar_b)
    total = jnp.zeros((8, 128), F32)
    for s in range(8):
        total = total + jnp.where(2 * s + row // 4 == mine, all_b[s], 0.0)

    def pick(i):
        return jnp.sum(jnp.where(kind == i, total, 0.0), axis=0, keepdims=True)

    mean = jnp.concatenate([pick(0), pick(1)], axis=1) / COUNT
    inv = lax.rsqrt(jnp.concatenate([pick(2), pick(3)], axis=1) / COUNT - mean * mean + 1e-05)

    def finish(b, _):
        v = (proj[b] - mean) * inv * pgain[...] + pshift[...]
        v = jnp.maximum(v, 0.0)
        for lane in range(2):
            rows[lane] = v[:, 128 * lane : 128 * (lane + 1)]
            for i in range(3):
                for k in range(2):
                    pair = rows[lane, pl.ds(64 * i + k, 32, stride=2), :]
                    tiles[lane, pl.ds(2 * i + k, 32, stride=8), :] = pair
        both = jnp.concatenate([tiles[0].reshape(32, 8, 128), tiles[1].reshape(32, 8, 128)], axis=1)
        sendbuf[pl.ds(32 * b, 32)] = both.astype(BF16)
        return 0

    tiles[...] = jnp.zeros(tiles.shape, F32)
    lax.fori_loop(0, 4, finish, 0)

    start = own * 32 + d
    slot = image * 2 + c
    pltpu.make_async_copy(sendbuf.at[start], out.at[slot], end_recv).start()

    def scatter(e, _):
        e = lax.rem(start + e, 128)
        remote(
            sendbuf.at[e], out.at[slot], end_send, end_recv, (lax.rem(e, 32), 2 * (e // 32) + parity)
        ).start()
        return 0

    lax.fori_loop(1, 128, scatter, 0)
    for cp in waits:
        cp.wait_send()
    for i in range(2):
        for h in range(2):
            is_self = jnp.logical_and(jnp.logical_and(c == z_hi, c == h), half == i)

            @pl.when(jnp.logical_not(is_self))
            def _():
                src = feat.at[i, pl.ds(3 * h, 3)]
                remote(src, xbuf.at[own], fs.at[2 * i + h], fr.at[own], sibling).wait_send()

    rest = sendbuf.at[pl.ds(0, 127)]
    pltpu.make_async_copy(rest, rest, end_send).wait()
    pltpu.make_async_copy(out, out, end_recv).wait()


def shards(
    features, first_w, second_w, third_w, point_w, pool_w, proj_w, gain, shift, pgain, pshift, group
):
    any_ = pl.BlockSpec(memory_space=pl.ANY)
    vmem = pl.BlockSpec(memory_space=pltpu.VMEM)
    smem = pl.BlockSpec(memory_space=pltpu.SMEM)
    dma = pltpu.SemaphoreType.DMA
    reduce_bufs = [
        pltpu.VMEM((n, rows, 128), F32) for rows in (32, 8) for n in (8, 7, 2, 3, 7, 8)
    ]
    out = pl.pallas_call(
        kernel,
        out_shape=jax.ShapeDtypeStruct((128, 16, 128), BF16),
        in_specs=[any_] * 4 + [vmem] * 7 + [smem],
        out_specs=any_,
        scratch_shapes=[
            pltpu.VMEM((27, 4, 4, 2, 32, 256), BF16),
            pltpu.VMEM((4, 3, 64, 1024), BF16),
            pltpu.VMEM((4, 3, 64, 1024), BF16),
            pltpu.VMEM((4, 3, 64, 1024), BF16),
            pltpu.VMEM((4, 3, 64, 1024), F32),
            pltpu.VMEM((4, 192, 256), F32),
            pltpu.VMEM((2, 192, 128), F32),
            pltpu.VMEM((2, 256, 128), F32),
            pltpu.VMEM((128, 16, 128), BF16),
            pltpu.VMEM((4, 8, 1024), F32),
            *reduce_bufs,
            dma((3,)), dma((CHUNKS, 12)), dma((CHUNKS, 12)), dma((4,)), dma((4,)), dma((3,)), dma((3,)),
            dma((24,)), dma((24,)), dma((24,)), dma((24,)), dma(()), dma(()),
        ],
        compiler_params=pltpu.CompilerParams(
            collective_id=0, has_side_effects=True, vmem_limit_bytes=56 << 20
        ),
        cost_estimate=pl.CostEstimate(flops=8_000_000_000, bytes_accessed=20_000_000, transcendentals=0),
    )(
        features, first_w.reshape(9, 32, 256), second_w.reshape(9, 32, 256), third_w.reshape(9, 32, 256),
        point_w, pool_w, proj_w, gain.reshape(1, -1), shift.reshape(1, -1),
        pgain.reshape(1, -1), pshift.reshape(1, -1), group,
    )
    out = out.reshape(64, 2, 2, 8, 128)[:, :, :, :6].reshape(64, 2, 2, 3, 2, 128)
    return out.transpose(0, 1, 3, 4, 2, 5).reshape(64, 6, 2, 256)


def solution(mesh):
    weight = P(None, None, "dp", None)
    in_specs = (P("dp", "rows", None, None), weight, weight, weight) + (P(),) * 8
    return jax.shard_map(
        shards, mesh=mesh, in_specs=in_specs, out_specs=P(None, "rows", "dp", None), check_vma=False
    )
```

time: 728 us -> 177 us (0.24)
  waiting for transfers between devices: 391 us -> 0 us
  blocking collectives: 241 us -> 0 us
  Pallas kernels: 0 us -> 172 us
  matrix products: 30.6 us -> 0 us
  starting transfers between devices: 25.1 us -> 0 us
  between operations: 13.6 us -> 0.02 us
  local copies, waits for them, and re-layouts: 16.8 us -> 5.16 us
  other arithmetic: 8.76 us -> 0 us
    psum x1 -> x0, waiting for transfers between devices: 238 us -> none  [shards(): lax.psum((group_first, group_second), ('dp', 'rows'))]
    psum x2 -> x0, blocking collectives: 223 us -> none  [the longest x1 147 us: shards(): pool_total = lax.psum(pool_part, 'rows')]
    pallas_call x0 -> x1, Pallas kernels: none -> 172 us  [shards(): pl.pallas_call(kernel, out_shape=jax.ShapeDtypeStruct((128, 16, 128), BF1...]
    all_gather x3 -> x0, waiting for transfers between devices: 151 us -> none  [the longest x1 90 us: shards(): lax.all_gather(second_atrous_weight, 'dp', axis=2, tiled=True)]
    dot_general x20 -> x0, matrix products: 30.6 us -> none  [the longest x9 22.8 us: row_tap_list(): jnp.einsum('irwc,kco->irwko', block_tensor, kernel_row_slice, preferred_e...]
    ppermute x6 -> x0, starting transfers between devices: 25 us -> none  [from_behind(): return lax.ppermute(array, axis, pairs)]
    all_to_all x1 -> x0, blocking collectives: 17.6 us -> none  [shards(): lax.all_to_all(local_out, 'dp', split_axis=2, concat_axis=0, tiled=True)]
    squeeze x9 -> x0, local copies, waits for them, and re-layouts: 8.76 us -> none  [row_tap_list(): partial_terms[:, :, :, 2]]
  transfers between devices with their start and end apart: 10 -> 0, of which waited for: 3 -> 0; matrix products, arithmetic and copies ran while one was open for 5% -> 0% of each run, Pallas kernels for 0% -> 0%
where the time goes in v1:
time: 177 us
  Pallas kernels  172 us (97%)
  local copies, waits for them, and re-layouts  5.16 us (3%)
    pallas_call x1, Pallas kernels, shards(): pl.pallas_call(kernel, out_shape=jax.ShapeDtypeStruct((128, 16, 128), BF1...  172 us
    unnamed x3, local copies, waits for them, and re-layouts  3.76 us

profile of v1, /device:TPU:1, one launch (start us, length us, event | category | flops | bytes accessed | tf_op | source)
XLA Modules:
  0.0 176.9 jit_solution(12282939582715776447)
XLA Ops:
  0.0 1.3 copy.21
  1.3 1.3 copy.22
  2.6 171.8 %shard_map.118 = bf16[128,16,128]{2,1,0:T(8,128)(2,1)} custom-call(bf16[2,6,64,1024]{3,2,1,0:T(8,128)(2,1)} %feat.1, bf16[9,32,256]{2,1,0:T(8,128)(2,1)} %bitcast.22, bf16[9,32,256]{2,1,0:T(8,128)(2,1)} %bitcast.23, bf16[9,32,256]{2,1,0:T(8,128)(2,1)} %bitcast.24, bf16[1024,256]{1,0:T(8,128)(2,1)} %point_w.1, bf16[1024,256]{1,0:T(8,128)(2,1)} %pool_w.1, ...), custom_call_target="tpu_custom_call" | custom-call | flops 8000000000 | bytes 20000000 | tf_op jit(solution)/shard_map/pallas_call | solution.py:396
  174.3 1.2 copy.20
  175.5 0.4 copy.18
  176.0 1.0 reshape.40

commit v2 on v1

--- a/solution.py
+++ b/solution.py
@@ -46,6 +46,7 @@
     y_pair = y + 1 - 2 * parity
     up, down = device(x, y, z + 1, c), device(x, y, z - 1, c)
     right, left = device(x + 1, y, z, c), device(x - 1, y, z, c)
+    y_up, y_down = device(x, y + 1, z, c), device(x, y - 1, z, c)
     sibling = device(x, y, z, other)
     pool_peers = (sibling, device(x, y_pair, z, c), device(x, y_pair, z, other))
 
@@ -57,7 +58,7 @@
         cp.start()
 
     barrier = pltpu.get_barrier_semaphore()
-    for peer in (up, down, right, left) + pool_peers:
+    for peer in (up, down, right, left, y_up, y_down, sibling, pool_peers[2]):
         pl.semaphore_signal(barrier, inc=1, device_id=peer, device_id_type=MESH)
     for b in range(4):
         src = device(x, 2 * (b % 2) + parity, (b // 2) * 4 + z_lo, z_hi)
@@ -68,11 +69,11 @@
 
     @pl.when(c == z_hi)
     def _():
-        pl.semaphore_wait(barrier, 10)
+        pl.semaphore_wait(barrier, 11)
 
     @pl.when(c != z_hi)
     def _():
-        pl.semaphore_wait(barrier, 11)
+        pl.semaphore_wait(barrier, 12)
 
     for cp in locals_:
         cp.wait()
@@ -85,8 +86,8 @@
         ref = wbuf.at[taps(k), zz, x, c]
         return ref if rows is None else wbuf.at[taps(k), zz, x, c, pl.ds(rows, 16)]
 
-    def column(k, xx, cc, zs=None):
-        return wbuf.at[taps(k), slice(None) if zs is None else pl.ds(zs, 2), xx, cc]
+    def column(k, xx, cc, zs=None, n=2):
+        return wbuf.at[taps(k), slice(None) if zs is None else pl.ds(zs, n), xx, cc]
 
     z_next, z_prev = lax.rem(z_lo + 1, 4), lax.rem(z_lo + 3, 4)
     z_far = lax.rem(z_lo + 2, 4)
@@ -105,33 +106,34 @@
     def arrived(ref, k, i):
         to(ref, k, i, sibling).wait_recv()
 
-    for k in range(2):
+    for k in range(CHUNKS):
         send(shard(k, z_lo), k, 0, up)
         send(shard(k, z_lo), k, 1, down)
 
-    for i in range(2):
-        for h in range(2):
-            src = feat.at[i, pl.ds(3 * h, 3)]
-            is_self = jnp.logical_and(jnp.logical_and(c == z_hi, c == h), half == i)
-
-            @pl.when(is_self)
-            def _():
-                pltpu.make_async_copy(src, xbuf.at[own], fr.at[own]).start()
-
-            @pl.when(jnp.logical_not(is_self))
-            def _():
-                remote(
-                    src, xbuf.at[own], fs.at[2 * i + h], fr.at[own],
-                    device(x, 2 * i + parity, c * 4 + z_lo, jnp.int32(h)),
-                ).start()
-
-    for k in range(2, CHUNKS):
-        send(shard(k, z_lo), k, 0, up)
-        send(shard(k, z_lo), k, 1, down)
+    def piece(i, h, row):
+        is_self = jnp.logical_and(jnp.logical_and(c == z_hi, c == h), half == i)
+        src, dst = feat.at[i, 3 * h + row], xbuf.at[own, row]
+        there = device(x, 2 * i + parity, c * 4 + z_lo, jnp.int32(h))
+        copy = remote(src, dst, fs.at[2 * i + h, row], fr.at[own, row], there)
+        return is_self, copy, lambda: pltpu.make_async_copy(src, dst, fr.at[own, row]).start()
+
+    def send_piece(i, h, row):
+        is_self, copy, local = piece(i, h, row)
+
+        @pl.when(is_self)
+        def _():
+            local()
+
+        @pl.when(jnp.logical_not(is_self))
+        def _():
+            copy.start()
+
+    pieces = [(i, h, row) for row in range(3) for i in range(2) for h in range(2)]
 
     def features_arrive():
         for b in range(4):
-            pltpu.make_async_copy(xbuf.at[b], xbuf.at[b], fr.at[b]).wait()
+            for row in range(3):
+                pltpu.make_async_copy(xbuf.at[b, row], xbuf.at[b, row], fr.at[b, row]).wait()
         part = jnp.zeros((8, 1024), F32)
         col = lax.broadcasted_iota(jnp.int32, (64, 1024), 0)
 
@@ -189,7 +191,8 @@
 
         lax.fori_loop(0, blocks, body, 0)
 
-    for t in range(CHUNKS + 4):
+    z_own, z_rest = 2 * parity, 2 - 2 * parity
+    for t in range(CHUNKS + 5):
         k = t
         if 0 <= k < CHUNKS:
             arrived(shard(k, z_prev), k, 0)
@@ -203,27 +206,37 @@
             send(column(k, x, c), k, 4, right)
             send(column(k, x, c), k, 5, left)
             send(column(k, x, c), k, 8, sibling)
+        for p in pieces[2 * t : 2 * t + 2]:
+            send_piece(*p)
         k = t - 2
         if 0 <= k < CHUNKS:
             arrived(column(k, x_prev, c), k, 4)
-            send(column(k, x_prev, c, 2), k, 6, right)
+            send(column(k, x_prev, c, z_own + 1, 1), k, 6, right)
             arrived(column(k, x_next, c), k, 5)
-            send(column(k, x_next, c, 0), k, 7, left)
+            send(column(k, x_next, c, z_own, 1), k, 7, left)
             send(column(k, x_prev, c), k, 9, sibling)
             send(column(k, x_next, c), k, 10, sibling)
         k = t - 3
         if 0 <= k < CHUNKS:
-            arrived(column(k, x_far, c, 2), k, 6)
-            arrived(column(k, x_far, c, 0), k, 7)
-            send(column(k, x_far, c), k, 11, sibling)
-        if t == 7:
+            arrived(column(k, x_far, c, z_own + 1, 1), k, 6)
+            arrived(column(k, x_far, c, z_own, 1), k, 7)
+            send(column(k, x_far, c, z_own, 1), k, 12, y_up)
+            send(column(k, x_far, c, z_own + 1, 1), k, 13, y_down)
+            send(column(k, x_far, c, z_own), k, 11, sibling)
+        k = t - 4
+        if 0 <= k < CHUNKS:
+            arrived(column(k, x_far, c, z_rest, 1), k, 12)
+            arrived(column(k, x_far, c, z_rest + 1, 1), k, 13)
+            send(column(k, x_far, c, z_rest), k, 14, sibling)
+        if t == 8:
             features_arrive()
-        for k in (2 * (t - 8), 2 * (t - 8) + 1):
+        for k in (2 * (t - 9), 2 * (t - 9) + 1):
             if 0 <= k < CHUNKS:
                 arrived(column(k, x, other), k, 8)
                 arrived(column(k, x_prev, other), k, 9)
                 arrived(column(k, x_next, other), k, 10)
-                arrived(column(k, x_far, other), k, 11)
+                arrived(column(k, x_far, other, z_own), k, 11)
+                arrived(column(k, x_far, other, z_rest), k, 14)
                 compute(k)
 
     for cp in sent:
@@ -306,10 +319,13 @@
     act = jnp.maximum(jnp.dot(pooled, pool_w[...], preferred_element_type=F32), 0.0).astype(BF16)
     pool_row = jnp.dot(act, proj_w[1024:1280], preferred_element_type=F32)[0:1]
 
+    gains = jnp.concatenate([gain[i : i + 1] for i in range(4)], axis=1)
+    shifts = jnp.concatenate([shift[i : i + 1] for i in range(4)], axis=1)
+
     def project(b, carry):
         first, second = carry
         v = acc[b].reshape(192, 1024)
-        v = (v - mean) * inv * gain[...] + shift[...]
+        v = (v - mean) * inv * gains + shifts
         v = jnp.maximum(v, 0.0).astype(BF16)
         p = jnp.dot(v, proj_w[0:1024], preferred_element_type=F32) + pool_row
         proj[b] = p
@@ -369,14 +385,12 @@
     lax.fori_loop(1, 128, scatter, 0)
     for cp in waits:
         cp.wait_send()
-    for i in range(2):
-        for h in range(2):
-            is_self = jnp.logical_and(jnp.logical_and(c == z_hi, c == h), half == i)
-
-            @pl.when(jnp.logical_not(is_self))
-            def _():
-                src = feat.at[i, pl.ds(3 * h, 3)]
-                remote(src, xbuf.at[own], fs.at[2 * i + h], fr.at[own], sibling).wait_send()
+    for p in pieces:
+        is_self, copy, _ = piece(*p)
+
+        @pl.when(jnp.logical_not(is_self))
+        def _():
+            copy.wait_send()
 
     rest = sendbuf.at[pl.ds(0, 127)]
     pltpu.make_async_copy(rest, rest, end_send).wait()
@@ -410,7 +424,7 @@
             pltpu.VMEM((128, 16, 128), BF16),
             pltpu.VMEM((4, 8, 1024), F32),
             *reduce_bufs,
-            dma((3,)), dma((CHUNKS, 12)), dma((CHUNKS, 12)), dma((4,)), dma((4,)), dma((3,)), dma((3,)),
+            dma((3,)), dma((CHUNKS, 15)), dma((CHUNKS, 15)), dma((4, 3)), dma((4, 3)), dma((3,)), dma((3,)),
             dma((24,)), dma((24,)), dma((24,)), dma((24,)), dma(()), dma(()),
         ],
         compiler_params=pltpu.CompilerParams(
@@ -419,7 +433,7 @@
         cost_estimate=pl.CostEstimate(flops=8_000_000_000, bytes_accessed=20_000_000, transcendentals=0),
     )(
         features, first_w.reshape(9, 32, 256), second_w.reshape(9, 32, 256), third_w.reshape(9, 32, 256),
-        point_w, pool_w, proj_w, gain.reshape(1, -1), shift.reshape(1, -1),
+        point_w, pool_w, proj_w, gain, shift,
         pgain.reshape(1, -1), pshift.reshape(1, -1), group,
     )
     out = out.reshape(64, 2, 2, 8, 128)[:, :, :, :6].reshape(64, 2, 2, 3, 2, 128)

time: 177 us -> 152 us (0.86)
  Pallas kernels: 172 us -> 149 us
  local copies, waits for them, and re-layouts: 5.16 us -> 2.6 us
    pallas_call x1, Pallas kernels: 172 us -> 149 us  [shards(): pl.pallas_call(kernel, out_shape=jax.ShapeDtypeStruct((128, 16, 128), BF1...]
    unnamed x3 -> x1, local copies, waits for them, and re-layouts: 3.76 us -> 1.2 us
where the time goes in v2:
time: 152 us
  Pallas kernels  149 us (98%)
  local copies, waits for them, and re-layouts  2.6 us (2%)
    pallas_call x1, Pallas kernels, shards(): pl.pallas_call(kernel, out_shape=jax.ShapeDtypeStruct((128, 16, 128), BF1...  149 us

profile of v2, /device:TPU:1, one launch (start us, length us, event | category | flops | bytes accessed | tf_op | source)
XLA Modules:
  0.0 151.6 jit_solution(14381798178683637198)
XLA Ops:
  0.0 148.9 %shard_map.118 = bf16[128,16,128]{2,1,0:T(8,128)(2,1)} custom-call(bf16[2,6,64,1024]{3,2,1,0:T(8,128)(2,1)} %feat.1, bf16[9,32,256]{2,1,0:T(8,128)(2,1)} %bitcast.12, bf16[9,32,256]{2,1,0:T(8,128)(2,1)} %bitcast.13, bf16[9,32,256]{2,1,0:T(8,128)(2,1)} %bitcast.14, bf16[1024,256]{1,0:T(8,128)(2,1)} %point_w.1, bf16[1024,256]{1,0:T(8,128)(2,1)} %pool_w.1, ...), custom_call_target="tpu_custom_call" | custom-call | flops 8000000000 | bytes 20000000 | tf_op jit(solution)/shard_map/pallas_call | solution.py:410
  148.9 1.2 copy.20
  150.1 0.4 copy.18
  150.6 1.0 reshape.32

commit v3 on v2

--- a/solution.py
+++ b/solution.py
@@ -12,6 +12,16 @@
 BF16 = jnp.bfloat16
 ORDER = ((0, 1), (1, 1), (2, 1), (0, 0), (0, 2), (1, 0), (1, 2), (2, 0), (2, 2))
 CHUNKS = len(ORDER)
+AHEAD = 4
+PER_STEP = (1, 1, 1, 1, 1, 2, 2, 2, 1)
+WORK = {
+    8: ((0, 1), ((0, 0, 2),)),
+    9: ((), ((1, 0, 2), (2, 0, 2))),
+    10: ((), ((3, 0, 2), (4, 0, 2))),
+    11: ((2,), ((0, 2, 1), (1, 2, 1))),
+    12: ((), ((2, 2, 1), (3, 2, 1), (4, 2, 1), (5, 0, 3), (6, 0, 3))),
+    13: ((), ((7, 0, 3), (8, 0, 3))),
+}
 COUNT = 4.0 * 48 * 64
 PIXELS = 48.0 * 64
 
@@ -30,7 +40,7 @@
 def kernel(
     feat, wa, wb, wc, point_w, pool_w, proj_w, gain, shift, pgain, pshift, group,
     out,
-    wbuf, xbuf, xright, xleft, acc, proj, rows, tiles, sendbuf, pool_buf,
+    wbuf, xbuf, xright, xleft, acc, proj, halves, tiles, sendbuf, pool_buf,
     msg_a, got_a, red_a, sum_y_a, sum_z_a, all_a,
     msg_b, got_b, red_b, sum_y_b, sum_z_b, all_b,
     local_sem, ws, wr, fs, fr, ps, pr, as_a, ar_a, as_b, ar_b, end_send, end_recv,
@@ -89,6 +99,9 @@
     def column(k, xx, cc, zs=None, n=2):
         return wbuf.at[taps(k), slice(None) if zs is None else pl.ds(zs, n), xx, cc]
 
+    def whole(k, cc):
+        return wbuf.at[taps(k), :, :, cc]
+
     z_next, z_prev = lax.rem(z_lo + 1, 4), lax.rem(z_lo + 3, 4)
     z_far = lax.rem(z_lo + 2, 4)
     x_next, x_prev, x_far = lax.rem(x + 1, 4), lax.rem(x + 3, 4), lax.rem(x + 2, 4)
@@ -106,9 +119,12 @@
     def arrived(ref, k, i):
         to(ref, k, i, sibling).wait_recv()
 
-    for k in range(CHUNKS):
+    def send_own(k):
         send(shard(k, z_lo), k, 0, up)
         send(shard(k, z_lo), k, 1, down)
+
+    for k in range(AHEAD):
+        send_own(k)
 
     def piece(i, h, row):
         is_self = jnp.logical_and(jnp.logical_and(c == z_hi, c == h), half == i)
@@ -130,83 +146,81 @@
 
     pieces = [(i, h, row) for row in range(3) for i in range(2) for h in range(2)]
 
-    def features_arrive():
+    col = lax.broadcasted_iota(jnp.int32, (64, 1024), 0)
+
+    def features_arrive(arriving):
+        first, count = arriving[0], len(arriving)
         for b in range(4):
-            for row in range(3):
+            for row in arriving:
                 pltpu.make_async_copy(xbuf.at[b, row], xbuf.at[b, row], fr.at[b, row]).wait()
-        part = jnp.zeros((8, 1024), F32)
-        col = lax.broadcasted_iota(jnp.int32, (64, 1024), 0)
-
-        def body(t, part):
-            v = xbuf[t // 3, lax.rem(t, 3)].astype(F32)
-            xright[t // 3, lax.rem(t, 3)] = jnp.where(col >= 4, pltpu.roll(v, 4, 0), 0.0).astype(BF16)
-            xleft[t // 3, lax.rem(t, 3)] = jnp.where(col < 60, pltpu.roll(v, 60, 0), 0.0).astype(BF16)
-            return part + v.reshape(8, 8, 1024).sum(axis=0)
-
-        pool_buf[0] = lax.fori_loop(0, 12, body, part)
-        for i, peer in enumerate(pool_peers):
-            remote(pool_buf.at[0], pool_buf.at[i + 1], ps.at[i], pr.at[i], peer).start()
-
-        def point(b, _):
-            acc[b, :, :, 0:256] = jnp.dot(
-                xbuf[b].reshape(192, 1024), point_w[...], preferred_element_type=F32
-            ).reshape(3, 64, 256)
-            return 0
-
-        lax.fori_loop(0, 4, point, 0)
-
-    def compute(k):
+
+        def body(b, part):
+            for row in arriving:
+                v = xbuf[b, row].astype(F32)
+                xright[b, row] = jnp.where(col >= 4, pltpu.roll(v, 4, 0), 0.0).astype(BF16)
+                xleft[b, row] = jnp.where(col < 60, pltpu.roll(v, 60, 0), 0.0).astype(BF16)
+                part = part + v.reshape(8, 8, 1024).sum(axis=0)
+            return part
+
+        part = jnp.zeros((8, 1024), F32) if first == 0 else pool_buf[0]
+        pool_buf[0] = lax.fori_loop(0, 4, body, part)
+        if arriving[-1] == 2:
+            for i, peer in enumerate(pool_peers):
+                remote(pool_buf.at[0], pool_buf.at[i + 1], ps.at[i], pr.at[i], peer).start()
+        acc[:, first : first + count, :, 0:256] = jnp.dot(
+            xbuf[:, first : first + count].reshape(count * 256, 1024), point_w[...],
+            preferred_element_type=F32,
+        ).reshape(4, count, 64, 256)
+
+    def compute(k, row, rows):
         branch, kh = ORDER[k]
         step = branch + 1
-        x0 = (0, 0, step)[kh]
-        o0 = (step, 0, 0)[kh]
-        blocks = 4 if kh == 1 else 4 - step
-        lanes = slice(256 * (branch + 1), 256 * (branch + 2))
-
-        def body(t, _):
-            b, o = x0 + t, o0 + t
-
-            def times(lhs, kw):
-                n = lhs.shape[1]
-                w = wbuf[9 * branch + 3 * kh + kw].reshape(1024, 256)
-                return jnp.dot(
-                    lhs.reshape(3 * n, 1024), w, preferred_element_type=F32
-                ).reshape(3, n, 256)
-
-            mid = times(xbuf[b], 1)
-            if kh == 1:
-                acc[o, :, :, lanes] = mid
-            else:
-                acc[o, :, :, lanes] += mid
-            if branch == 0:
-                acc[o, :, 8:64, lanes] += times(xright[b], 0)[:, 0:56]
-                acc[o, :, 0:56, lanes] += times(xleft[b], 2)[:, 8:64]
-            elif branch == 1:
-                acc[o, :, 24:64, lanes] += times(xbuf[b, :, 0:48], 0)[:, 0:40]
-                acc[o, :, 0:40, lanes] += times(xbuf[b, :, 16:64], 2)[:, 8:48]
-            else:
-                acc[o, :, 32:64, lanes] += times(xright[b, :, 0:32], 0)
-                acc[o, :, 0:32, lanes] += times(xleft[b, :, 32:64], 2)
-            return 0
-
-        lax.fori_loop(0, blocks, body, 0)
-
+        n = 4 if kh == 1 else 4 - step
+        src = (pl.ds((0, 0, step)[kh], n), pl.ds(row, rows))
+        dst = (pl.ds((step, 0, 0)[kh], n), pl.ds(row, rows))
+        lanes = pl.ds(256 * (branch + 1), 256)
+
+        def times(lhs, kw):
+            m = lhs.shape[2]
+            w = wbuf[9 * branch + 3 * kh + kw].reshape(1024, 256)
+            return jnp.dot(
+                lhs.reshape(n * rows * m, 1024), w, preferred_element_type=F32
+            ).reshape(n, rows, m, 256)
+
+        mid = times(xbuf[src], 1)
+        if kh == 1:
+            acc[*dst, :, lanes] = mid
+        else:
+            acc[*dst, :, lanes] += mid
+        if branch == 0:
+            acc[*dst, 8:64, lanes] += times(xright[src], 0)[:, :, 0:56]
+            acc[*dst, 0:56, lanes] += times(xleft[src], 2)[:, :, 8:64]
+        elif branch == 1:
+            acc[*dst, 24:64, lanes] += times(xbuf[*src, 0:48], 0)[:, :, 0:40]
+            acc[*dst, 0:40, lanes] += times(xbuf[*src, 16:64], 2)[:, :, 8:48]
+        else:
+            acc[*dst, 32:64, lanes] += times(xright[*src, 0:32], 0)
+            acc[*dst, 0:32, lanes] += times(xleft[*src, 32:64], 2)
+
+    here = set()
     z_own, z_rest = 2 * parity, 2 - 2 * parity
     for t in range(CHUNKS + 5):
-        k = t
-        if 0 <= k < CHUNKS:
-            arrived(shard(k, z_prev), k, 0)
-            send(shard(k, z_prev, 16), k, 2, up)
-            arrived(shard(k, z_next), k, 1)
-            send(shard(k, z_next, 0), k, 3, down)
+        for k in (2 * t, 2 * t + 1):
+            if k < CHUNKS:
+                arrived(shard(k, z_prev), k, 0)
+                send(shard(k, z_prev, 16), k, 2, up)
+                arrived(shard(k, z_next), k, 1)
+                send(shard(k, z_next, 0), k, 3, down)
+            if k + AHEAD < CHUNKS:
+                send_own(k + AHEAD)
         k = t - 1
         if 0 <= k < CHUNKS:
             arrived(shard(k, z_far, 16), k, 2)
             arrived(shard(k, z_far, 0), k, 3)
             send(column(k, x, c), k, 4, right)
             send(column(k, x, c), k, 5, left)
-            send(column(k, x, c), k, 8, sibling)
-        for p in pieces[2 * t : 2 * t + 2]:
+        done = sum(PER_STEP[:t])
+        for p in pieces[done : done + sum(PER_STEP[t : t + 1])]:
             send_piece(*p)
         k = t - 2
         if 0 <= k < CHUNKS:
@@ -214,30 +228,25 @@
             send(column(k, x_prev, c, z_own + 1, 1), k, 6, right)
             arrived(column(k, x_next, c), k, 5)
             send(column(k, x_next, c, z_own, 1), k, 7, left)
-            send(column(k, x_prev, c), k, 9, sibling)
-            send(column(k, x_next, c), k, 10, sibling)
         k = t - 3
         if 0 <= k < CHUNKS:
             arrived(column(k, x_far, c, z_own + 1, 1), k, 6)
             arrived(column(k, x_far, c, z_own, 1), k, 7)
-            send(column(k, x_far, c, z_own, 1), k, 12, y_up)
-            send(column(k, x_far, c, z_own + 1, 1), k, 13, y_down)
-            send(column(k, x_far, c, z_own), k, 11, sibling)
+            send(column(k, x_far, c, z_own, 1), k, 9, y_up)
+            send(column(k, x_far, c, z_own + 1, 1), k, 10, y_down)
         k = t - 4
         if 0 <= k < CHUNKS:
-            arrived(column(k, x_far, c, z_rest, 1), k, 12)
-            arrived(column(k, x_far, c, z_rest + 1, 1), k, 13)
-            send(column(k, x_far, c, z_rest), k, 14, sibling)
-        if t == 8:
-            features_arrive()
-        for k in (2 * (t - 9), 2 * (t - 9) + 1):
-            if 0 <= k < CHUNKS:
-                arrived(column(k, x, other), k, 8)
-                arrived(column(k, x_prev, other), k, 9)
-                arrived(column(k, x_next, other), k, 10)
-                arrived(column(k, x_far, other, z_own), k, 11)
-                arrived(column(k, x_far, other, z_rest), k, 14)
-                compute(k)
+            arrived(column(k, x_far, c, z_rest, 1), k, 9)
+            arrived(column(k, x_far, c, z_rest + 1, 1), k, 10)
+            send(whole(k, c), k, 8, sibling)
+        arriving, work = WORK.get(t, ((), ()))
+        if arriving:
+            features_arrive(arriving)
+        for k, row, rows in work:
+            if k not in here:
+                here.add(k)
+                arrived(whole(k, other), k, 8)
+            compute(k, row, rows)
 
     for cp in sent:
         cp.wait_send()
@@ -359,10 +368,10 @@
         v = (proj[b] - mean) * inv * pgain[...] + pshift[...]
         v = jnp.maximum(v, 0.0)
         for lane in range(2):
-            rows[lane] = v[:, 128 * lane : 128 * (lane + 1)]
+            halves[lane] = v[:, 128 * lane : 128 * (lane + 1)]
             for i in range(3):
                 for k in range(2):
-                    pair = rows[lane, pl.ds(64 * i + k, 32, stride=2), :]
+                    pair = halves[lane, pl.ds(64 * i + k, 32, stride=2), :]
                     tiles[lane, pl.ds(2 * i + k, 32, stride=8), :] = pair
         both = jnp.concatenate([tiles[0].reshape(32, 8, 128), tiles[1].reshape(32, 8, 128)], axis=1)
         sendbuf[pl.ds(32 * b, 32)] = both.astype(BF16)
@@ -424,7 +433,7 @@
             pltpu.VMEM((128, 16, 128), BF16),
             pltpu.VMEM((4, 8, 1024), F32),
             *reduce_bufs,
-            dma((3,)), dma((CHUNKS, 15)), dma((CHUNKS, 15)), dma((4, 3)), dma((4, 3)), dma((3,)), dma((3,)),
+            dma((3,)), dma((CHUNKS, 11)), dma((CHUNKS, 11)), dma((4, 3)), dma((4, 3)), dma((3,)), dma((3,)),
             dma((24,)), dma((24,)), dma((24,)), dma((24,)), dma(()), dma(()),
         ],
         compiler_params=pltpu.CompilerParams(

time: 152 us -> 137 us (0.901)
  Pallas kernels: 149 us -> 135 us
    pallas_call x1, Pallas kernels: 149 us -> 135 us  [shards(): pl.pallas_call(kernel, out_shape=jax.ShapeDtypeStruct((128, 16, 128), BF1...]
where the time goes in v3:
time: 137 us
  Pallas kernels  135 us (99%)
  local copies, waits for them, and re-layouts  2.6 us (2%)
    pallas_call x1, Pallas kernels, shards(): pl.pallas_call(kernel, out_shape=jax.ShapeDtypeStruct((128, 16, 128), BF1...  135 us

profile of v3, /device:TPU:1, one launch (start us, length us, event | category | flops | bytes accessed | tf_op | source)
XLA Modules:
  0.0 137.3 jit_solution(15970578858640697222)
XLA Ops:
  0.0 134.7 %shard_map.118 = bf16[128,16,128]{2,1,0:T(8,128)(2,1)} custom-call(bf16[2,6,64,1024]{3,2,1,0:T(8,128)(2,1)} %feat.1, bf16[9,32,256]{2,1,0:T(8,128)(2,1)} %bitcast.12, bf16[9,32,256]{2,1,0:T(8,128)(2,1)} %bitcast.13, bf16[9,32,256]{2,1,0:T(8,128)(2,1)} %bitcast.14, bf16[1024,256]{1,0:T(8,128)(2,1)} %point_w.1, bf16[1024,256]{1,0:T(8,128)(2,1)} %pool_w.1, ...), custom_call_target="tpu_custom_call" | custom-call | flops 8000000000 | bytes 20000000 | tf_op jit(solution)/shard_map/pallas_call | solution.py:419
  134.7 1.2 copy.20
  135.9 0.4 copy.18
  136.3 1.0 reshape.32

commit v4 on v3

--- a/solution.py
+++ b/solution.py
@@ -12,7 +12,7 @@
 BF16 = jnp.bfloat16
 ORDER = ((0, 1), (1, 1), (2, 1), (0, 0), (0, 2), (1, 0), (1, 2), (2, 0), (2, 2))
 CHUNKS = len(ORDER)
-AHEAD = 4
+AHEAD = 6
 PER_STEP = (1, 1, 1, 1, 1, 2, 2, 2, 1)
 WORK = {
     8: ((0, 1), ((0, 0, 2),)),
@@ -38,9 +38,9 @@
 
 
 def kernel(
-    feat, wa, wb, wc, point_w, pool_w, proj_w, gain, shift, pgain, pshift, group,
+    feat, wa, wb, wc, point_hbm, pool_hbm, proj_hbm, gain, shift, pgain, pshift, group,
     out,
-    wbuf, xbuf, xright, xleft, acc, proj, halves, tiles, sendbuf, pool_buf,
+    wbuf, point_w, pool_w, proj_w, xbuf, xright, xleft, acc, proj, halves, tiles, sendbuf, pool_buf,
     msg_a, got_a, red_a, sum_y_a, sum_z_a, all_a,
     msg_b, got_b, red_b, sum_y_b, sum_z_b, all_b,
     local_sem, ws, wr, fs, fr, ps, pr, as_a, ar_a, as_b, ar_b, end_send, end_recv,
@@ -64,9 +64,14 @@
         pltpu.make_async_copy(w, wbuf.at[pl.ds(9 * i, 9), z_lo, x, c], local_sem.at[i])
         for i, w in enumerate((wa, wb, wc))
     ]
-    for cp in locals_:
+    dense = [
+        pltpu.make_async_copy(src, dst, local_sem.at[3 + i])
+        for i, (src, dst) in enumerate(((point_hbm, point_w), (pool_hbm, pool_w), (proj_hbm, proj_w)))
+    ]
+    for cp in locals_ + dense:
         cp.start()
 
+    tiles[...] = jnp.zeros(tiles.shape, F32)
     barrier = pltpu.get_barrier_semaphore()
     for peer in (up, down, right, left, y_up, y_down, sibling, pool_peers[2]):
         pl.semaphore_signal(barrier, inc=1, device_id=peer, device_id_type=MESH)
@@ -204,6 +209,7 @@
 
     here = set()
     z_own, z_rest = 2 * parity, 2 - 2 * parity
+    z_first, z_given, z_missing = parity, 3 * parity, 3 - 3 * parity
     for t in range(CHUNKS + 5):
         for k in (2 * t, 2 * t + 1):
             if k < CHUNKS:
@@ -217,17 +223,19 @@
         if 0 <= k < CHUNKS:
             arrived(shard(k, z_far, 16), k, 2)
             arrived(shard(k, z_far, 0), k, 3)
-            send(column(k, x, c), k, 4, right)
-            send(column(k, x, c), k, 5, left)
+            send(column(k, x, c, z_first, 3), k, 4, right)
+            send(column(k, x, c, z_first, 3), k, 5, left)
         done = sum(PER_STEP[:t])
         for p in pieces[done : done + sum(PER_STEP[t : t + 1])]:
             send_piece(*p)
         k = t - 2
         if 0 <= k < CHUNKS:
-            arrived(column(k, x_prev, c), k, 4)
+            arrived(column(k, x_prev, c, z_first, 3), k, 4)
             send(column(k, x_prev, c, z_own + 1, 1), k, 6, right)
-            arrived(column(k, x_next, c), k, 5)
+            arrived(column(k, x_next, c, z_first, 3), k, 5)
             send(column(k, x_next, c, z_own, 1), k, 7, left)
+            send(column(k, x_prev, c, z_given, 1), k, 11, y_up)
+            send(column(k, x_next, c, z_given, 1), k, 12, y_down)
         k = t - 3
         if 0 <= k < CHUNKS:
             arrived(column(k, x_far, c, z_own + 1, 1), k, 6)
@@ -238,8 +246,13 @@
         if 0 <= k < CHUNKS:
             arrived(column(k, x_far, c, z_rest, 1), k, 9)
             arrived(column(k, x_far, c, z_rest + 1, 1), k, 10)
+            arrived(column(k, x_prev, c, z_missing, 1), k, 11)
+            arrived(column(k, x_next, c, z_missing, 1), k, 12)
             send(whole(k, c), k, 8, sibling)
         arriving, work = WORK.get(t, ((), ()))
+        if t == 6:
+            for cp in dense:
+                cp.wait()
         if arriving:
             features_arrive(arriving)
         for k, row, rows in work:
@@ -364,7 +377,7 @@
     mean = jnp.concatenate([pick(0), pick(1)], axis=1) / COUNT
     inv = lax.rsqrt(jnp.concatenate([pick(2), pick(3)], axis=1) / COUNT - mean * mean + 1e-05)
 
-    def finish(b, _):
+    def finish(b):
         v = (proj[b] - mean) * inv * pgain[...] + pshift[...]
         v = jnp.maximum(v, 0.0)
         for lane in range(2):
@@ -375,23 +388,23 @@
                     tiles[lane, pl.ds(2 * i + k, 32, stride=8), :] = pair
         both = jnp.concatenate([tiles[0].reshape(32, 8, 128), tiles[1].reshape(32, 8, 128)], axis=1)
         sendbuf[pl.ds(32 * b, 32)] = both.astype(BF16)
-        return 0
-
-    tiles[...] = jnp.zeros(tiles.shape, F32)
-    lax.fori_loop(0, 4, finish, 0)
-
-    start = own * 32 + d
+
+
     slot = image * 2 + c
-    pltpu.make_async_copy(sendbuf.at[start], out.at[slot], end_recv).start()
-
-    def scatter(e, _):
-        e = lax.rem(start + e, 128)
+
+    def scatter(e, b):
+        e = lax.rem(d + e, 32)
         remote(
-            sendbuf.at[e], out.at[slot], end_send, end_recv, (lax.rem(e, 32), 2 * (e // 32) + parity)
+            sendbuf.at[32 * b + e], out.at[slot], end_send, end_recv, (e, 2 * b + parity)
         ).start()
-        return 0
-
-    lax.fori_loop(1, 128, scatter, 0)
+        return b
+
+    for turn in range(4):
+        b = lax.rem(own + turn, 4)
+        finish(b)
+        if turn == 0:
+            pltpu.make_async_copy(sendbuf.at[32 * own + d], out.at[slot], end_recv).start()
+        lax.fori_loop(1 if turn == 0 else 0, 32, scatter, b)
     for cp in waits:
         cp.wait_send()
     for p in pieces:
@@ -419,10 +432,13 @@
     out = pl.pallas_call(
         kernel,
         out_shape=jax.ShapeDtypeStruct((128, 16, 128), BF16),
-        in_specs=[any_] * 4 + [vmem] * 7 + [smem],
+        in_specs=[any_] * 7 + [vmem] * 4 + [smem],
         out_specs=any_,
         scratch_shapes=[
             pltpu.VMEM((27, 4, 4, 2, 32, 256), BF16),
+            pltpu.VMEM((1024, 256), BF16),
+            pltpu.VMEM((1024, 256), BF16),
+            pltpu.VMEM((1280, 256), BF16),
             pltpu.VMEM((4, 3, 64, 1024), BF16),
             pltpu.VMEM((4, 3, 64, 1024), BF16),
             pltpu.VMEM((4, 3, 64, 1024), BF16),
@@ -433,7 +449,7 @@
             pltpu.VMEM((128, 16, 128), BF16),
             pltpu.VMEM((4, 8, 1024), F32),
             *reduce_bufs,
-            dma((3,)), dma((CHUNKS, 11)), dma((CHUNKS, 11)), dma((4, 3)), dma((4, 3)), dma((3,)), dma((3,)),
+            dma((6,)), dma((CHUNKS, 13)), dma((CHUNKS, 13)), dma((4, 3)), dma((4, 3)), dma((3,)), dma((3,)),
             dma((24,)), dma((24,)), dma((24,)), dma((24,)), dma(()), dma(()),
         ],
         compiler_params=pltpu.CompilerParams(

time: 137 us -> 135 us (0.985)
  Pallas kernels: 135 us -> 133 us
    pallas_call x1, Pallas kernels: 135 us -> 133 us  [shards(): pl.pallas_call(kernel, out_shape=jax.ShapeDtypeStruct((128, 16, 128), BF1...]
where the time goes in v4:
time: 135 us
  Pallas kernels  133 us (99%)
  local copies, waits for them, and re-layouts  2.6 us (2%)
    pallas_call x1, Pallas kernels, shards(): pl.pallas_call(kernel, out_shape=jax.ShapeDtypeStruct((128, 16, 128), BF1...  133 us

profile of v4, /device:TPU:1, one launch (start us, length us, event | category | flops | bytes accessed | tf_op | source)
XLA Modules:
  0.0 135.2 jit_solution(5560279784178521433)
XLA Ops:
  0.0 132.6 %shard_map.118 = bf16[128,16,128]{2,1,0:T(8,128)(2,1)} custom-call(bf16[2,6,64,1024]{3,2,1,0:T(8,128)(2,1)} %feat.1, bf16[9,32,256]{2,1,0:T(8,128)(2,1)} %bitcast.12, bf16[9,32,256]{2,1,0:T(8,128)(2,1)} %bitcast.13, bf16[9,32,256]{2,1,0:T(8,128)(2,1)} %bitcast.14, bf16[1024,256]{1,0:T(8,128)(2,1)} %point_hbm.1, bf16[1024,256]{1,0:T(8,128)(2,1)} %pool_hbm.1, ...), custom_call_target="tpu_custom_call" | custom-call | flops 8000000000 | bytes 20000000 | tf_op jit(solution)/shard_map/pallas_call | solution.py:432
  132.6 1.2 copy.20
  133.8 0.4 copy.18
  134.2 1.0 reshape.32
